TPU v7x, 512 devices: a whole 4x8x8 slice. The times are simulated.
512 devices in a mesh: bank: 128 (over y, z, x_hi), tm: 4 (over x_lo, core).
Axes of the slice: x: 4 (x_hi: 2, x_lo: 2; x = x_hi * 2 + x_lo), y: 8, z: 8, core: 2. Of those that a mesh axis runs over, the one named last changes fastest.
Arguments:
- strain: float32 [3, 4, 16384], P(None, 'tm', 'bank'), may hold values from -6 to 6
- fir_taps: float32 [4096], replicated, may hold values from -0.09375 to 0.09375
- templates: bfloat16 [256, 2, 2048], P('bank'), may hold values from -6 to 6
Outputs:
- snr_sq: float32 [3, 256, 65536], P(None, 'bank', 'tm')
- loudest: float32 [3, 65536], P(None, 'tm')
All inputs are finite; a program needn't handle non-finite values.
Results may differ from a plain program's by a relative error of at most 0.003.
Values may be sent and summed in bfloat16 or wider, within the bound.
A program may use at most 64 MiB of HBM per device.

v0:
```python
import jax
import jax.numpy as jnp
from jax import lax
from jax.sharding import PartitionSpec as P


def with_halo(block, sides, width):
    for axis, dim in sides:
        count = lax.axis_size(axis)
        forward = [(i, i + 1) for i in range(count - 1)]
        forward.append((count - 1, 0))
        backward = [(target, source) for source, target in forward]
        low = lax.ppermute(
            lax.slice_in_dim(block, block.shape[dim] - width, None, axis=dim), axis, forward
        )
        high = lax.ppermute(lax.slice_in_dim(block, 0, width, axis=dim), axis, backward)
        block = jnp.concatenate([low, block, high], axis=dim)
    return block


def toeplitz_table(filt, reach_count):
    filters, span_len = filt.shape
    lane_count = 128
    cycle_len = lane_count * reach_count + lane_count
    padded_filt = jnp.pad(filt, ((0, 0), (0, cycle_len - span_len)))
    tiled = jnp.tile(padded_filt, (1, lane_count))[:, : lane_count * (cycle_len - 1)]
    return tiled.reshape(filters, lane_count, cycle_len - 1)[:, :, : lane_count * reach_count]


def slide(signals, table, span_len, precision):
    row_count, length = signals.shape
    filters = table.shape[0]
    lane_count = 128
    reach_count = table.shape[2] // lane_count
    out_len = length - span_len + 1
    frames = (out_len + lane_count - 1) // lane_count
    full_len = lane_count * (frames + reach_count)
    signals = jnp.pad(signals, ((0, 0), (0, full_len - length)))
    framed = signals.reshape(row_count, frames + reach_count, lane_count)
    windows = jnp.concatenate(
        [framed[:, offset : offset + frames] for offset in range(reach_count)], axis=2
    )
    result = lax.dot_general(
        windows,
        table,
        (((2,), (2,)), ((), ())),
        preferred_element_type=jnp.float32,
        precision=precision,
    )
    result = jnp.transpose(result, (0, 2, 1, 3)).reshape(row_count, filters, frames * lane_count)
    return result[:, :, :out_len]


def reach_of(span_len):
    return (span_len + 127 + 127) // 128


def whiten_rows(signal, fir_taps):
    tap_count = fir_taps.shape[0]
    table = toeplitz_table(fir_taps.reshape(1, tap_count), reach_of(tap_count))
    return slide(signal, table, tap_count, lax.Precision.HIGHEST)[:, 0, :]


def shards(strain, fir_taps, templates):
    stretch_part = strain[:, 0, :]
    gathered = lax.all_gather(stretch_part, "bank", axis=1, tiled=True)
    stretch_len = gathered.shape[1]
    tmpl_len = templates.shape[2]
    tap_count = fir_taps.shape[0]
    margin = tap_count // 2 + tmpl_len // 2
    extended = with_halo(gathered, (("tm", 1),), margin)
    white_len = stretch_len + tmpl_len - 1
    whitened = whiten_rows(extended[:, : white_len + tap_count - 1], fir_taps).astype(jnp.bfloat16)
    tmpl_dev = templates.shape[0]
    bank_rows = templates.reshape(tmpl_dev * 2, tmpl_len)
    bank_table = toeplitz_table(bank_rows, reach_of(tmpl_len))
    energy = jnp.mean(jnp.square(templates.astype(jnp.float32)), axis=(1, 2)) + 1e-06
    divisor = tmpl_len * energy
    result = slide(whitened, bank_table, tmpl_len, None)
    result = result.reshape(whitened.shape[0], tmpl_dev, 2, stretch_len)
    snr_sq = jnp.sum(result * result, axis=2) / divisor[None, :, None]
    top_power = lax.pmax(jnp.max(snr_sq, axis=1), "bank")
    return (snr_sq, top_power)


def solution(mesh):
    in_specs = (P(None, "tm", "bank"), P(), P("bank", None, None))
    out_specs = (P(None, "bank", "tm"), P(None, "tm"))
    return jax.shard_map(shards, mesh=mesh, in_specs=in_specs, out_specs=out_specs, check_vma=False)
```

profile of v0, /device:TPU:16, one launch (start us, length us, event | category | flops | bytes accessed | tf_op | source)
XLA Modules:
  0.0 1681.6 jit_solution(14929333578318406595)
XLA Ops:
  7.2 0.0 all-reduce.6.cloned.1.call-start
  7.2 321.0 %all-gather = f32[3,1,16384]{2,1,0:T(1,128)S(1)} all-gather(f32[3,1,128]{2,1,0:T(1,128)} %param.3), channel_id=2, replica_groups=mesh['bank'=128,'tm'=4] {'bank'}, dimensions={2}, use_global_device_ids=true | all-gather | bytes 198144 | tf_op jit(solution)/shard_map/all_gather | solution.py:66
  328.2 0.1 copy.10
  328.3 1.9 collective-permute-start
  330.3 3.6 collective-permute-start.1
  333.9 0.7 reshape.49
  334.6 0.8 multiply_reduce_fusion
  335.5 0.8 pad_reduce_fusion
  336.2 0.1 broadcast_bitcast_fusion.1
  336.4 2.3 copy.7
  338.7 24.4 %slice_reduce_fusion = f32[556928]{0:T(1024)} fusion(f32[1,557056]{1,0:T(1,128)S(1)} %bitcast.41), kind=kLoop, calls=%fused_computation.2 | loop fusion | bytes 4455424 | tf_op jit(solution)/shard_map/slice | solution.py:26
  363.1 0.2 broadcast_bitcast_fusion
  363.3 4.5 reshape.46
  367.8 1.8 copy.8
  369.7 2.3 slice.288
  372.0 3.3 reshape.57
  375.3 6.0 reshape.50
  381.3 0.0 collective-permute-done
  381.3 0.1 select_maximum_fusion
  381.4 0.1 reshape.44
  382.4 0.7 copy-done
  383.1 6.2 fusion.9
  389.4 0.1 slice_bitcast_fusion.10
  389.5 0.1 pad.18
  389.6 0.1 reshape.48
  390.5 1.1 fusion.6
  391.6 0.5 mul.18
  392.1 1.2 reduce_sum.18
  393.3 1.8 fusion.10
  395.1 0.0 all-reduce.6.cloned.1.call-update
  395.1 1277.9 %all-reduce.6.cloned.1.call-done = f32[3,16384]{1,0:T(4,128)} async-done(((f32[3,16384]{1,0:T(4,128)}), f32[3,16384]{1,0:T(4,128)}) %all-reduce.6.cloned.1.call-update) | async-done | bytes 196624 | tf_op jit(solution)/shard_map/pmax | solution.py:82
  1673.0 1.7 copy.60
  (58 shorter events, 1.4 us)
Async XLA Ops:
  7.2 1665.9 %all-reduce.6.cloned.1.call-start = ((), (), s32[]{:S(2)}) async-start(), calls=%async_computation | async-start | bytes 524288 | tf_op jit(solution)/shard_map/pmax | solution.py:82
  328.3 52.9 %collective-permute-start = (f32[3,3072]{1,0:T(4,128)S(1)}, f32[3,3072]{1,0:T(4,128)S(1)}, u32[]{:S(2)}, u32[]{:S(2)}) collective-permute-start(f32[3,3072]{1,0:T(4,128)S(1)} %get-tuple-element.4), channel_id=1, source_target_pairs={{0,1},{1,2},{2,3},{3,0},{4,5},{5,6},{6,7},{7,4},{8,9},{9,10},{10,1... | collective-permute-start | bytes 110600 | tf_op jit(solution)/shard_map/ppermute | solution.py:13
  330.3 51.0 %collective-permute-start.1 = (f32[3,3072]{1,0:T(4,128)S(1)}, f32[3,3072]{1,0:T(4,128)S(1)}, u32[]{:S(2)}, u32[]{:S(2)}) collective-permute-start(f32[3,3072]{1,0:T(4,128)S(1)} %get-tuple-element.5), channel_id=1, source_target_pairs={{1,0},{2,1},{3,2},{0,3},{5,4},{6,5},{7,6},{4,7},{9,8},{10,9},{11,1... | collective-permute-start | bytes 110600 | tf_op jit(solution)/shard_map/ppermute | solution.py:16
  381.5 1.6 copy-start
  382.4 8.1 copy-start.1
Sparse Core Ops, SparseCore 0:
  395.3 1277.7 all-reduce.5
where the time goes:
time: 1680 us
  waiting for transfers between devices  1280 us (76%)
  blocking collectives  321 us (19%)
  local copies, waits for them, and re-layouts  51.3 us (3%)
    pmax x1, waiting for transfers between devices, shards(): top_power = lax.pmax(jnp.max(snr_sq, axis=1), 'bank')  1280 us
    all_gather x1, blocking collectives, shards(): gathered = lax.all_gather(stretch_part, 'bank', axis=1, tiled=True)  321 us
  transfers between devices with their start and end apart: 3, of which 1 were waited for; matrix products, arithmetic and copies ran while one was open for 3% of the time, Pallas kernels for 0%

commit v1 on v0

v1 whole, which is shorter than its diff:
```python
import jax
import jax.numpy as jnp
from jax import lax
from jax.experimental import pallas as pl
from jax.experimental.pallas import tpu as pltpu
from jax.sharding import PartitionSpec as P

MESH = pl.DeviceIdType.MESH
LANES = 128
DET = 3
NY, NZ, NX, NT = 8, 8, 2, 4
BANK = NY * NZ * NX
TAPS = 4096
TLEN = 2048
WSTEP = 5
WOFF = 17
CSTEP = 8
COFF = 17


def far_first(i):
    half = (i + 1) // 2
    odd = i % 2
    return 4 + half - 2 * half * odd


def kernel(
    strain, taps, tmpl, snr, loud,
    gath, tap_v, tmpl_v, wtab, ctab, xh, xl, white, cwin, sbuf, rbuf, res,
    in_sem, send_sem, recv_sem, halo_sem,
):
    b = lax.axis_index("bank")
    m = lax.axis_index("tm")
    y, z, x = b // 16, (b // 2) % 8, b % 2
    up, down = (m + 1) % NT, (m + NT - 1) % NT
    pairs = gath.reshape(96, 2, 8, LANES)

    def bank_of(yy, zz, xx):
        return yy * 16 + zz * 2 + xx

    barrier = pltpu.get_barrier_semaphore()

    def greet(dev):
        pl.semaphore_signal(barrier, inc=1, device_id=dev, device_id_type=MESH)

    for j in range(1, NZ):
        greet((bank_of(y, (z + j) % NZ, x), m))
    for j in range(1, NY * NX):
        jy, jx = far_first((j - 1) // 2), j % 2
        greet((bank_of((y + jy) % NY, z, (x + jx) % NX), m))
    for yy in (0, 1):
        for xx in range(NX):
            greet((bank_of(yy, z, xx), up))
    for yy in (6, 7):
        for xx in range(NX):
            greet((bank_of(yy, z, xx), down))

    own_row = pairs.at[12 + 8 * y + z, x, pl.ds(0, DET), :]
    load_own = pltpu.make_async_copy(strain.at[:, 0, :], own_row, in_sem.at[0])
    load_taps = pltpu.make_async_copy(taps, tap_v, in_sem.at[1])
    load_tmpl = pltpu.make_async_copy(tmpl, tmpl_v, in_sem.at[2])
    load_own.start()
    load_taps.start()
    load_tmpl.start()
    load_own.wait()
    load_taps.wait()
    load_tmpl.wait()

    row_id = lax.broadcasted_iota(jnp.int32, (LANES, LANES), 0)
    lane_id = lax.broadcasted_iota(jnp.int32, (LANES, LANES), 1)
    keep = lane_id >= row_id
    zero = jnp.zeros((LANES, LANES), jnp.float32)
    zero_b = jnp.zeros((LANES, LANES), jnp.bfloat16)

    def skew(row):
        wide = jnp.broadcast_to(row, (LANES, LANES))
        return pltpu.roll(wide, 0, 1, stride=1, stride_axis=0)

    def tap_table():
        last = zero
        for c in range(TAPS // LANES + 1):
            if c < TAPS // LANES:
                now = skew(tap_v[pl.ds(c, 1), :])
            else:
                now = zero
            tile = jnp.where(keep, now, last)
            last = now
            hi = tile.astype(jnp.bfloat16)
            lo = (tile - hi.astype(jnp.float32)).astype(jnp.bfloat16)
            for part, val in enumerate((hi, lo)):
                wtab[part, 0:128, c * 128:(c + 1) * 128] = val
                wtab[part, 128:256, (c + 1) * 128:(c + 2) * 128] = val
        for part in range(2):
            wtab[part, 0:128, 33 * 128:34 * 128] = zero_b
            wtab[part, 128:256, 0:128] = zero_b

    def tmpl_table(f):
        last = zero
        rows = tmpl_v[f // 2].astype(jnp.float32)
        for c in range(TLEN // LANES + 1):
            if c < TLEN // LANES:
                now = skew(rows[f % 2:f % 2 + 1, c * 128:(c + 1) * 128])
            else:
                now = zero
            ctab[f * 128:(f + 1) * 128, c * 128:(c + 1) * 128] = jnp.where(keep, now, last).astype(jnp.bfloat16)
            last = now

    edge = jnp.where((y <= 1) | (y >= 6), NY * NX, 0)
    pl.semaphore_wait(barrier, (NZ - 1) + (NY * NX - 1) + edge)

    for j in (4, 3, 5, 2, 6, 1, 7):
        pltpu.make_async_remote_copy(
            src_ref=own_row, dst_ref=own_row, send_sem=send_sem.at[0], recv_sem=recv_sem.at[0],
            device_id=(bank_of(y, (z + j) % NZ, x), m), device_id_type=MESH,
        ).start()
    tap_table()
    got = pairs.at[pl.ds(0, NZ - 1), 0, pl.ds(0, DET), :]
    pltpu.make_async_copy(got, got, recv_sem.at[0]).wait()

    group = pairs.at[pl.ds(12 + 8 * y, 8), x, pl.ds(0, DET), :]
    for i in range(NY * NX - 1):
        jy, jx = far_first(i // 2), 1 - i % 2
        pltpu.make_async_remote_copy(
            src_ref=group, dst_ref=group, send_sem=send_sem.at[1], recv_sem=recv_sem.at[1],
            device_id=(bank_of((y + jy) % NY, z, (x + jx) % NX), m), device_id_type=MESH,
        ).start()

    def margin(cond, src_at, dst_at, count, to):
        @pl.when(cond)
        def _():
            for i in range(NY * NX):
                jy, jx = far_first(i // 2), 1 - i % 2
                pltpu.make_async_remote_copy(
                    src_ref=pairs.at[pl.ds(src_at, count), x, pl.ds(0, DET), :],
                    dst_ref=pairs.at[pl.ds(dst_at, count), x, pl.ds(0, DET), :],
                    send_sem=halo_sem.at[0], recv_sem=recv_sem.at[1],
                    device_id=(bank_of((y + jy) % NY, z, (x + jx) % NX), to), device_id_type=MESH,
                ).start()

    margin(y == 0, 12, 76, 8, down)
    margin(y == 1, 20, 84, 4, down)
    margin(y == 6, 64, 0, 4, up)
    margin(y == 7, 68, 4, 8, up)

    for f in range(4):
        tmpl_table(f)
    inv = []
    for k in range(2):
        wide = tmpl_v[k].astype(jnp.float32)
        energy = jnp.sum(wide * wide, keepdims=True) / (2.0 * TLEN) + 1e-6
        inv.append(1.0 / (TLEN * energy))

    got = pairs.at[pl.ds(0, 84), :, pl.ds(0, DET), :]
    pltpu.make_async_copy(got, got, recv_sem.at[1]).wait()

    for d in range(DET):
        for a in range(WSTEP + WOFF - 1):
            for h in range(2):
                val = gath[pl.ds(8 * (2 * a + h) + d, 16, stride=16 * WSTEP), :]
                hi = val.astype(jnp.bfloat16)
                lo = (val - hi.astype(jnp.float32)).astype(jnp.bfloat16)
                for o in range(WOFF):
                    if 0 <= a - o < WSTEP:
                        lanes = slice(o * 256 + h * 128, o * 256 + h * 128 + 128)
                        xh[(a - o) * 16:(a - o + 1) * 16, lanes] = hi
                        xl[(a - o) * 16:(a - o + 1) * 16, lanes] = lo
        nt = (((1,), (1,)), ((), ()))
        hi_all = xh[...]
        out = lax.dot_general(hi_all, wtab[0], nt, preferred_element_type=jnp.float32)
        out += lax.dot_general(hi_all, wtab[1], nt, preferred_element_type=jnp.float32)
        out += lax.dot_general(xl[...], wtab[0], nt, preferred_element_type=jnp.float32)
        for a in range(WSTEP):
            for h in range(2):
                white[pl.ds(2 * a + h, 16, stride=2 * WSTEP), :] = out[a * 16:(a + 1) * 16, h * 128:(h + 1) * 128]
        for a in range(CSTEP + COFF - 1):
            val = white[pl.ds(a, 16, stride=CSTEP), :].astype(jnp.bfloat16)
            for o in range(COFF):
                if 0 <= a - o < CSTEP:
                    cwin[(a - o) * 16:(a - o + 1) * 16, o * 128:(o + 1) * 128] = val
        corr = lax.dot_general(cwin[...], ctab[...], nt, preferred_element_type=jnp.float32)
        power = []
        for k in range(2):
            c0 = corr[:, k * 256:k * 256 + 128]
            c1 = corr[:, k * 256 + 128:k * 256 + 256]
            power.append((c0 * c0 + c1 * c1) * inv[k])
        best = jnp.maximum(power[0], power[1])
        for a in range(CSTEP):
            rows = slice(a * 16, (a + 1) * 16)
            for k in range(2):
                snr[pl.ds(d * 256 + 2 * a + k, 16, stride=16), :] = power[k][rows]
            sbuf[pl.ds(8 * a + d, 16, stride=64), :] = best[rows]

    send3 = sbuf.reshape(BANK, 8, LANES)

    def scatter(i, carry):
        jx = 1 - i // 64
        jy, jz = far_first((i // 8) % 8), far_first(i % 8)
        p = bank_of((y + jy) % NY, (z + jz) % NZ, (x + jx) % NX)
        pltpu.make_async_remote_copy(
            src_ref=send3.at[p, pl.ds(0, DET), :], dst_ref=rbuf.at[b, pl.ds(0, DET), :],
            send_sem=send_sem.at[2], recv_sem=recv_sem.at[2],
            device_id=(p, m), device_id_type=MESH,
        ).start()
        return carry

    lax.fori_loop(0, BANK - 1, scatter, 0)
    own = send3[b, 0:DET, :]
    got = rbuf.at[pl.ds(0, BANK - 1), pl.ds(0, DET), :]
    pltpu.make_async_copy(got, got, recv_sem.at[2]).wait()
    rbuf[b, 0:DET, :] = own
    top = jnp.max(rbuf[:, 0:DET, :], axis=0)
    res[...] = top
    mine = pl.ds(pl.multiple_of(b * 128, 128), 128)

    def spread(i, carry):
        jx = 1 - i // 64
        jy, jz = far_first((i // 8) % 8), far_first(i % 8)
        p = bank_of((y + jy) % NY, (z + jz) % NZ, (x + jx) % NX)
        pltpu.make_async_remote_copy(
            src_ref=res, dst_ref=loud.at[:, mine],
            send_sem=send_sem.at[3], recv_sem=recv_sem.at[3],
            device_id=(p, m), device_id_type=MESH,
        ).start()
        return carry

    lax.fori_loop(0, BANK - 1, spread, 0)
    loud[:, mine] = top
    got = rbuf.at[pl.ds(0, BANK - 1), pl.ds(0, DET), :]
    pltpu.make_async_copy(got, got, recv_sem.at[3]).wait()
    sent = pairs.at[pl.ds(0, NZ - 1), 0, pl.ds(0, DET), :]
    pltpu.make_async_copy(sent, sent, send_sem.at[0]).wait()
    sent = pairs.at[pl.ds(0, 60), :, pl.ds(0, DET), :]
    pltpu.make_async_copy(sent, sent, send_sem.at[1]).wait()

    @pl.when((y == 0) | (y == 7))
    def _():
        part = pairs.at[pl.ds(0, 64), :, pl.ds(0, DET), :]
        pltpu.make_async_copy(part, part, halo_sem.at[0]).wait()

    @pl.when((y == 1) | (y == 6))
    def _():
        part = pairs.at[pl.ds(0, 32), :, pl.ds(0, DET), :]
        pltpu.make_async_copy(part, part, halo_sem.at[0]).wait()

    sent = rbuf.at[pl.ds(0, BANK - 1), pl.ds(0, DET), :]
    pltpu.make_async_copy(sent, sent, send_sem.at[2]).wait()
    pltpu.make_async_copy(sent, sent, send_sem.at[3]).wait()


def shards(strain, fir_taps, templates):
    any_spec = pl.BlockSpec(memory_space=pl.ANY)
    vmem_spec = pl.BlockSpec(memory_space=pltpu.VMEM)
    snr, loud = pl.pallas_call(
        kernel,
        out_shape=(
            jax.ShapeDtypeStruct((DET * 256, LANES), jnp.float32),
            jax.ShapeDtypeStruct((DET, BANK * LANES), jnp.float32),
        ),
        in_specs=[any_spec, any_spec, any_spec],
        out_specs=(vmem_spec, vmem_spec),
        scratch_shapes=[
            pltpu.VMEM((96 * 16, LANES), jnp.float32),
            pltpu.VMEM((TAPS // LANES, LANES), jnp.float32),
            pltpu.VMEM((2, 2, TLEN), jnp.bfloat16),
            pltpu.VMEM((2, 256, WOFF * 256), jnp.bfloat16),
            pltpu.VMEM((512, COFF * 128), jnp.bfloat16),
            pltpu.VMEM((WSTEP * 16, WOFF * 256), jnp.bfloat16),
            pltpu.VMEM((WSTEP * 16, WOFF * 256), jnp.bfloat16),
            pltpu.VMEM((160, LANES), jnp.float32),
            pltpu.VMEM((CSTEP * 16, COFF * 128), jnp.bfloat16),
            pltpu.VMEM((BANK * 8, LANES), jnp.float32),
            pltpu.VMEM((BANK, 8, LANES), jnp.float32),
            pltpu.VMEM((DET, LANES), jnp.float32),
            pltpu.SemaphoreType.DMA((3,)),
            pltpu.SemaphoreType.DMA((4,)),
            pltpu.SemaphoreType.DMA((4,)),
            pltpu.SemaphoreType.DMA((1,)),
        ],
        compiler_params=pltpu.CompilerParams(
            collective_id=0, has_side_effects=True, vmem_limit_bytes=32 * 1024 * 1024
        ),
        name="matched_filter",
    )(strain, fir_taps.reshape(TAPS // LANES, LANES), templates)
    snr = snr.reshape(DET, 128, 2, LANES).transpose(0, 2, 1, 3).reshape(DET, 2, 128 * LANES)
    return snr, loud


def solution(mesh):
    in_specs = (P(None, "tm", "bank"), P(), P("bank", None, None))
    out_specs = (P(None, "bank", "tm"), P(None, "tm"))
    return jax.shard_map(shards, mesh=mesh, in_specs=in_specs, out_specs=out_specs, check_vma=False)
```

time: 1680 us -> 69.9 us (0.04)
  the two profiles are of different devices: /device:TPU:16 before, /device:TPU:1 now
where the time goes in v1:
time: 69.9 us; the launch traced here: 69.5 us
  Pallas kernels  65.3 us (93%)
  local copies, waits for them, and re-layouts  3.56 us (5%)
    pallas_call x1, Pallas kernels, shards(): pl.pallas_call(kernel, out_shape=(jax.ShapeDtypeStruct((DET * 256, LANES)...  65.3 us
    unnamed x8, local copies, waits for them, and re-layouts  3.56 us

profile of v1, /device:TPU:1, one launch (start us, length us, event | category | flops | bytes accessed | tf_op | source)
XLA Modules:
  0.0 69.5 jit_solution(17250611950885057478)
XLA Ops:
  0.6 0.0 copy-start.2
  0.6 0.7 copy-done.2
  1.3 0.0 copy-start
  1.3 0.7 %copy-done = f32[4096]{0:T(1024)S(1)} copy-done((f32[4096]{0:T(1024)S(1)}, f32[4096]{0:T(1024)}, u32[]{:S(2)}) %copy-start) | copy-done | bytes 16408
  2.0 0.0 copy-start.1
  2.0 0.7 %copy-done.1 = bf16[2,2,2048]{2,1,0:T(2,128)(2,1)S(1)} copy-done((bf16[2,2,2048]{2,1,0:T(2,128)(2,1)S(1)}, bf16[2,2,2048]{2,1,0:T(2,128)(2,1)}, u32[]{:S(2)}) %copy-start.1) | copy-done | bytes 16408
  2.7 65.3 %matched_filter.1 = (f32[768,128]{1,0:T(8,128)S(1)}, f32[3,16384]{1,0:T(4,128)S(1)}) custom-call(f32[3,1,128]{2,1,0:T(1,128)S(1)} %copy-done.2, f32[32,128]{1,0:T(8,128)S(1)} %bitcast.7, bf16[2,2,2048]{2,1,0:T(2,128)(2,1)S(1)} %copy-done.1), custom_call_target="tpu_custom_call" | custom-call | tf_op jit(solution)/shard_map/matched_filter/pallas_call | solution.py:253
  68.1 0.7 %copy.8 = f32[3,2,16384]{2,1,0:T(2,128)} copy(f32[3,2,16384]{2,1,0:T(2,128)S(1)} %bitcast.6) | data formatting | bytes 786432
  68.8 0.7 %copy.9 = f32[3,16384]{1,0:T(4,128)} copy(f32[3,16384]{1,0:T(4,128)S(1)} %get-tuple-element.9) | data formatting | bytes 393216
Async XLA Ops:
  0.6 0.7 copy-start.2
  1.3 0.7 %copy-start = (f32[4096]{0:T(1024)S(1)}, f32[4096]{0:T(1024)}, u32[]{:S(2)}) copy-start(f32[4096]{0:T(1024)} %param.4) | copy-start | bytes 49156
  2.0 0.7 %copy-start.1 = (bf16[2,2,2048]{2,1,0:T(2,128)(2,1)S(1)}, bf16[2,2,2048]{2,1,0:T(2,128)(2,1)}, u32[]{:S(2)}) copy-start(bf16[2,2,2048]{2,1,0:T(2,128)(2,1)} %tmpl.1) | copy-start | bytes 49156

commit v2 on v1

v2 whole, which is shorter than its diff:
```python
import jax
import jax.numpy as jnp
from jax import lax
from jax.experimental import pallas as pl
from jax.experimental.pallas import tpu as pltpu
from jax.sharding import PartitionSpec as P

MESH = pl.DeviceIdType.MESH
LANES = 128
DET = 3
NY, NZ, NX, NT = 8, 8, 2, 4
BANK = NY * NZ * NX
TAPS = 4096
TLEN = 2048
WSTEP = 5
WOFF = 17
CSTEP = 8
COFF = 17
ROWS = 16 * DET


def far_first(i):
    half = (i + 1) // 2
    odd = i % 2
    return 4 + half - 2 * half * odd


def kernel(
    strain, taps, tmpl, snr, loud,
    gath, tap_v, tmpl_v, wtab, ctab, xh, xl, white, cwin, sbuf, rbuf, res,
    in_sem, send_sem, recv_sem, halo_sem,
):
    b = lax.axis_index("bank")
    m = lax.axis_index("tm")
    y, z, x = b // 16, (b // 2) % 8, b % 2
    up, down = (m + 1) % NT, (m + NT - 1) % NT
    pairs = gath.reshape(96, 2, 8, LANES)

    def bank_of(yy, zz, xx):
        return yy * 16 + zz * 2 + xx

    barrier = pltpu.get_barrier_semaphore()

    def greet(dev):
        pl.semaphore_signal(barrier, inc=1, device_id=dev, device_id_type=MESH)

    for j in range(1, 8):
        jj = far_first(j - 1)
        greet((bank_of((y + jj) % NY, z, 1 - x), m))
        greet((bank_of(y, (z + jj) % NZ, 1 - x), m))
        greet((bank_of((y + jj) % NY, z, x), m))
        greet((bank_of(y, (z + jj) % NZ, x), m))
    greet((bank_of(y, z, 1 - x), m))
    for j in range(NZ):
        greet((bank_of(y, j, x), up))
        greet((bank_of(y, j, x), down))
    for yy in (0, 1):
        greet((bank_of(yy, z, x), up))
        greet((bank_of(6 + yy, z, x), down))

    own_row = pairs.at[12 + 8 * y + z, x, pl.ds(0, DET), :]
    load_own = pltpu.make_async_copy(strain.at[:, 0, :], own_row, in_sem.at[0])
    load_taps = pltpu.make_async_copy(taps, tap_v, in_sem.at[1])
    load_tmpl = pltpu.make_async_copy(tmpl, tmpl_v, in_sem.at[2])
    load_own.start()
    load_taps.start()
    load_tmpl.start()
    load_own.wait()
    load_taps.wait()
    load_tmpl.wait()

    row_id = lax.broadcasted_iota(jnp.int32, (LANES, LANES), 0)
    lane_id = lax.broadcasted_iota(jnp.int32, (LANES, LANES), 1)
    keep = lane_id >= row_id
    zero = jnp.zeros((LANES, LANES), jnp.float32)
    zero_b = jnp.zeros((LANES, LANES), jnp.bfloat16)

    def skew(row):
        wide = jnp.broadcast_to(row, (LANES, LANES))
        return pltpu.roll(wide, 0, 1, stride=1, stride_axis=0)

    def tap_table():
        last = zero
        for c in range(TAPS // LANES + 1):
            if c < TAPS // LANES:
                now = skew(tap_v[pl.ds(c, 1), :])
            else:
                now = zero
            tile = jnp.where(keep, now, last)
            last = now
            hi = tile.astype(jnp.bfloat16)
            lo = (tile - hi.astype(jnp.float32)).astype(jnp.bfloat16)
            for part, val in enumerate((hi, lo)):
                wtab[part, 0:128, c * 128:(c + 1) * 128] = val
                wtab[part, 128:256, (c + 1) * 128:(c + 2) * 128] = val
        for part in range(2):
            wtab[part, 0:128, 33 * 128:34 * 128] = zero_b
            wtab[part, 128:256, 0:128] = zero_b

    def tmpl_table(f):
        last = zero
        rows = tmpl_v[f // 2].astype(jnp.float32)
        for c in range(TLEN // LANES + 1):
            if c < TLEN // LANES:
                now = skew(rows[f % 2:f % 2 + 1, c * 128:(c + 1) * 128])
            else:
                now = zero
            ctab[f * 128:(f + 1) * 128, c * 128:(c + 1) * 128] = jnp.where(keep, now, last).astype(jnp.bfloat16)
            last = now

    edge = jnp.where((y <= 1) | (y >= 6), NY, 0)
    pl.semaphore_wait(barrier, 29 + 2 * NZ + edge)

    def send_a(p):
        pltpu.make_async_remote_copy(
            src_ref=own_row, dst_ref=own_row, send_sem=send_sem.at[0], recv_sem=recv_sem.at[0],
            device_id=(p, m), device_id_type=MESH,
        ).start()

    for j in range(15):
        jj, dx = far_first(j // 2), 1 - j % 2
        send_a(jnp.where(
            x == 0, bank_of((y + jj) % NY, z, (x + dx) % NX), bank_of(y, (z + jj) % NZ, (x + dx) % NX)
        ))
    tap_table()
    got = pairs.at[pl.ds(0, 15), 0, pl.ds(0, DET), :]
    pltpu.make_async_copy(got, got, recv_sem.at[0]).wait()

    def send_b(src, dst, sem, p, to):
        pltpu.make_async_remote_copy(
            src_ref=src, dst_ref=dst, send_sem=sem, recv_sem=recv_sem.at[1],
            device_id=(p, to), device_id_type=MESH,
        ).start()

    eights = gath.reshape(12, 8, 2, 8, LANES)
    at_q, at_r = (12 + z) // 8, (z + 4) % 8
    yline = eights.at[pl.ds(at_q, 8), at_r, 0, pl.ds(0, DET), :]
    zline = pairs.at[pl.ds(12 + 8 * y, 8), 1, pl.ds(0, DET), :]
    for j in range(7):
        jj = far_first(j)
        send_b(yline, yline, send_sem.at[1], bank_of(y, (z + jj) % NZ, x), m)
        send_b(zline, zline, send_sem.at[1], bank_of((y + jj) % NY, z, x), m)

    def margin_y(cond, src_at, dst_at, count, to):
        @pl.when(cond)
        def _():
            for j in range(NY):
                send_b(
                    pairs.at[pl.ds(src_at, count), 1, pl.ds(0, DET), :],
                    pairs.at[pl.ds(dst_at, count), 1, pl.ds(0, DET), :],
                    halo_sem.at[0], bank_of((y + far_first(j)) % NY, z, x), to,
                )

    margin_y(y == 0, 12, 76, 8, down)
    margin_y(y == 1, 20, 84, 4, down)
    margin_y(y == 6, 64, 0, 4, up)
    margin_y(y == 7, 68, 4, 8, up)

    def margin_z(cond, low, high):
        @pl.when(cond)
        def _():
            for j in range(NZ):
                p = bank_of(y, (z + far_first(j)) % NZ, x)
                send_b(
                    eights.at[pl.ds(at_q, low), at_r, 0, pl.ds(0, DET), :],
                    eights.at[pl.ds(at_q + 8, low), at_r, 0, pl.ds(0, DET), :],
                    halo_sem.at[1], p, down,
                )
                send_b(
                    eights.at[pl.ds(8, high), at_r, 0, pl.ds(0, DET), :],
                    eights.at[pl.ds(0, high), at_r, 0, pl.ds(0, DET), :],
                    halo_sem.at[1], p, up,
                )

    margin_z(z < 4, 2, 1)
    margin_z(z >= 4, 1, 2)

    for f in range(4):
        tmpl_table(f)
    inv = []
    for k in range(2):
        wide = tmpl_v[k].astype(jnp.float32)
        energy = jnp.sum(wide * wide, keepdims=True) / (2.0 * TLEN) + 1e-6
        inv.append(1.0 / (TLEN * energy))

    got = pairs.at[pl.ds(0, 80), :, pl.ds(0, DET), :]
    pltpu.make_async_copy(got, got, recv_sem.at[1]).wait()

    nt = (((1,), (1,)), ((), ()))
    for a in range(WSTEP + WOFF - 1):
        for d in range(DET):
            rows = slice(a * ROWS + d * 16, a * ROWS + d * 16 + 16)
            for h in range(2):
                val = gath[pl.ds(8 * (2 * a + h) + d, 16, stride=16 * WSTEP), :]
                hi = val.astype(jnp.bfloat16)
                lo = (val - hi.astype(jnp.float32)).astype(jnp.bfloat16)
                xh[rows, h * 128:(h + 1) * 128] = hi
                xl[rows, h * 128:(h + 1) * 128] = lo
    hi_all = jnp.concatenate([xh[o * ROWS:(o + WSTEP) * ROWS, :] for o in range(WOFF)], axis=1)
    lo_all = jnp.concatenate([xl[o * ROWS:(o + WSTEP) * ROWS, :] for o in range(WOFF)], axis=1)
    both = lax.dot_general(
        jnp.concatenate([hi_all, lo_all], axis=0), wtab[0], nt, preferred_element_type=jnp.float32
    )
    out = both[:WSTEP * ROWS] + both[WSTEP * ROWS:]
    out += lax.dot_general(hi_all, wtab[1], nt, preferred_element_type=jnp.float32)
    for a in range(WSTEP):
        for d in range(DET):
            rows = slice(a * ROWS + d * 16, a * ROWS + d * 16 + 16)
            for h in range(2):
                white[pl.ds(d * 160 + 2 * a + h, 16, stride=2 * WSTEP), :] = out[rows, h * 128:(h + 1) * 128]

    for a in range(CSTEP + COFF - 1):
        for d in range(DET):
            rows = slice(a * ROWS + d * 16, a * ROWS + d * 16 + 16)
            cwin[rows, :] = white[pl.ds(d * 160 + a, 16, stride=CSTEP), :].astype(jnp.bfloat16)
    wins = jnp.concatenate([cwin[o * ROWS:(o + CSTEP) * ROWS, :] for o in range(COFF)], axis=1)
    corr = lax.dot_general(wins, ctab[...], nt, preferred_element_type=jnp.float32)
    power = []
    for k in range(2):
        c0 = corr[:, k * 256:k * 256 + 128]
        c1 = corr[:, k * 256 + 128:k * 256 + 256]
        power.append((c0 * c0 + c1 * c1) * inv[k])
    best = jnp.maximum(power[0], power[1])
    for a in range(CSTEP):
        for d in range(DET):
            rows = slice(a * ROWS + d * 16, a * ROWS + d * 16 + 16)
            for k in range(2):
                snr[pl.ds(d * 256 + 2 * a + k, 16, stride=16), :] = power[k][rows]
            sbuf[pl.ds(8 * a + d, 16, stride=64), :] = best[rows]

    send3 = sbuf.reshape(BANK, 8, LANES)

    far = (4, 3, 5, 2, 6, 1, 7, 0)
    zs = [((z + jz) % NZ) * 2 for jz in far]

    def to_all(make):
        def some(i, carry):
            jx, jy = 1 - i // 8, far_first(i % 8)
            base = bank_of((y + jy) % NY, 0, (x + jx) % NX)
            for n in range(8):
                make(base + zs[n]).start()
            return carry

        lax.fori_loop(0, 15, some, 0)
        base = bank_of(y, 0, x)
        for n in range(7):
            make(base + zs[n]).start()

    to_all(lambda p: pltpu.make_async_remote_copy(
        src_ref=send3.at[p, pl.ds(0, DET), :], dst_ref=rbuf.at[b, pl.ds(0, DET), :],
        send_sem=send_sem.at[2], recv_sem=recv_sem.at[2],
        device_id=(p, m), device_id_type=MESH,
    ))
    own = send3[b, 0:DET, :]
    got = rbuf.at[pl.ds(0, BANK - 1), pl.ds(0, DET), :]
    pltpu.make_async_copy(got, got, recv_sem.at[2]).wait()
    rbuf[b, 0:DET, :] = own
    top = jnp.max(rbuf[:, 0:DET, :], axis=0)
    res[...] = top
    mine = pl.ds(pl.multiple_of(b * 128, 128), 128)

    to_all(lambda p: pltpu.make_async_remote_copy(
        src_ref=res, dst_ref=loud.at[:, mine],
        send_sem=send_sem.at[3], recv_sem=recv_sem.at[3],
        device_id=(p, m), device_id_type=MESH,
    ))
    loud[:, mine] = top
    got = rbuf.at[pl.ds(0, BANK - 1), pl.ds(0, DET), :]
    pltpu.make_async_copy(got, got, recv_sem.at[3]).wait()
    sent = pairs.at[pl.ds(0, 15), 0, pl.ds(0, DET), :]
    pltpu.make_async_copy(sent, sent, send_sem.at[0]).wait()
    sent = pairs.at[pl.ds(0, 56), :, pl.ds(0, DET), :]
    pltpu.make_async_copy(sent, sent, send_sem.at[1]).wait()
    part = pairs.at[pl.ds(0, 12), :, pl.ds(0, DET), :]
    pltpu.make_async_copy(part, part, halo_sem.at[1]).wait()

    @pl.when((y == 0) | (y == 7))
    def _():
        part = pairs.at[pl.ds(0, 32), :, pl.ds(0, DET), :]
        pltpu.make_async_copy(part, part, halo_sem.at[0]).wait()

    @pl.when((y == 1) | (y == 6))
    def _():
        part = pairs.at[pl.ds(0, 16), :, pl.ds(0, DET), :]
        pltpu.make_async_copy(part, part, halo_sem.at[0]).wait()

    sent = rbuf.at[pl.ds(0, BANK - 1), pl.ds(0, DET), :]
    pltpu.make_async_copy(sent, sent, send_sem.at[2]).wait()
    pltpu.make_async_copy(sent, sent, send_sem.at[3]).wait()


def shards(strain, fir_taps, templates):
    any_spec = pl.BlockSpec(memory_space=pltpu.HBM)
    vmem_spec = pl.BlockSpec(memory_space=pltpu.VMEM)
    snr, loud = pl.pallas_call(
        kernel,
        out_shape=(
            jax.ShapeDtypeStruct((DET * 256, LANES), jnp.float32),
            jax.ShapeDtypeStruct((DET, BANK * LANES), jnp.float32),
        ),
        in_specs=[any_spec, any_spec, any_spec],
        out_specs=(vmem_spec, vmem_spec),
        scratch_shapes=[
            pltpu.VMEM((96 * 16, LANES), jnp.float32),
            pltpu.VMEM((TAPS // LANES, LANES), jnp.float32),
            pltpu.VMEM((2, 2, TLEN), jnp.bfloat16),
            pltpu.VMEM((2, 256, WOFF * 256), jnp.bfloat16),
            pltpu.VMEM((512, COFF * 128), jnp.bfloat16),
            pltpu.VMEM(((WSTEP + WOFF - 1) * ROWS, 256), jnp.bfloat16),
            pltpu.VMEM(((WSTEP + WOFF - 1) * ROWS, 256), jnp.bfloat16),
            pltpu.VMEM((DET * 160, LANES), jnp.float32),
            pltpu.VMEM(((CSTEP + COFF - 1) * ROWS, LANES), jnp.bfloat16),
            pltpu.VMEM((BANK * 8, LANES), jnp.float32),
            pltpu.VMEM((BANK, 8, LANES), jnp.float32),
            pltpu.VMEM((DET, LANES), jnp.float32),
            pltpu.SemaphoreType.DMA((3,)),
            pltpu.SemaphoreType.DMA((4,)),
            pltpu.SemaphoreType.DMA((4,)),
            pltpu.SemaphoreType.DMA((2,)),
        ],
        compiler_params=pltpu.CompilerParams(
            collective_id=0, has_side_effects=True, vmem_limit_bytes=32 * 1024 * 1024
        ),
        name="matched_filter",
    )(*[pltpu.with_memory_space_constraint(v, pltpu.HBM) for v in (strain, fir_taps.reshape(TAPS // LANES, LANES), templates)])
    snr = snr.reshape(DET, 128, 2, LANES).transpose(0, 2, 1, 3).reshape(DET, 2, 128 * LANES)
    return snr, loud


def solution(mesh):
    in_specs = (P(None, "tm", "bank"), P(), P("bank", None, None))
    out_specs = (P(None, "bank", "tm"), P(None, "tm"))
    return jax.shard_map(shards, mesh=mesh, in_specs=in_specs, out_specs=out_specs, check_vma=False)
```

time: 69.9 us -> 51.9 us (0.74)
  Pallas kernels: 65.3 us -> 49.6 us
  local copies, waits for them, and re-layouts: 3.56 us -> 1.45 us
    pallas_call x1, Pallas kernels: 65.3 us -> 49.6 us  [shards(): pl.pallas_call(kernel, out_shape=(jax.ShapeDtypeStruct((DET * 256, LANES)...]
    unnamed x8 -> x2, local copies, waits for them, and re-layouts: 3.56 us -> 1.45 us
where the time goes in v2:
time: 51.9 us; the launch traced here: 51.7 us
  Pallas kernels  49.6 us (96%)
  local copies, waits for them, and re-layouts  1.45 us (3%)
  between operations  0.64 us (1%)
    pallas_call x1, Pallas kernels, shards(): pl.pallas_call(kernel, out_shape=(jax.ShapeDtypeStruct((DET * 256, LANES)...  49.6 us
    unnamed x2, local copies, waits for them, and re-layouts  1.45 us

profile of v2, /device:TPU:1, one launch (start us, length us, event | category | flops | bytes accessed | tf_op | source)
XLA Modules:
  0.0 51.7 jit_solution(2997974481992595790)
XLA Ops:
  0.6 49.6 %matched_filter.1 = (f32[768,128]{1,0:T(8,128)S(1)}, f32[3,16384]{1,0:T(4,128)S(1)}) custom-call(f32[3,1,128]{2,1,0:T(1,128)} %strain.1, f32[32,128]{1,0:T(8,128)} %bitcast.7, bf16[2,2,2048]{2,1,0:T(2,128)(2,1)} %tmpl.1), custom_call_target="tpu_custom_call" | custom-call | tf_op jit(solution)/shard_map/matched_filter/pallas_call | solution.py:295
  50.3 0.7 %copy.8 = f32[3,2,16384]{2,1,0:T(2,128)} copy(f32[3,2,16384]{2,1,0:T(2,128)S(1)} %bitcast.6) | data formatting | bytes 786432
  51.0 0.7 %copy.9 = f32[3,16384]{1,0:T(4,128)} copy(f32[3,16384]{1,0:T(4,128)S(1)} %get-tuple-element.9) | data formatting | bytes 393216

commit v3 on v2

--- a/solution.py
+++ b/solution.py
@@ -14,8 +14,7 @@
 TLEN = 2048
 WSTEP = 5
 WOFF = 17
-CSTEP = 8
-COFF = 17
+COFF = 9
 ROWS = 16 * DET
 
 
@@ -27,7 +26,7 @@
 
 def kernel(
     strain, taps, tmpl, snr, loud,
-    gath, tap_v, tmpl_v, wtab, ctab, xh, xl, white, cwin, sbuf, rbuf, res,
+    gath, tap_v, tmpl_v, wtab, ctab, xh, xl, acc, cwin, sbuf, rbuf, res,
     in_sem, send_sem, recv_sem, halo_sem,
 ):
     b = lax.axis_index("bank")
@@ -100,14 +99,22 @@
     def tmpl_table(f):
         last = zero
         rows = tmpl_v[f // 2].astype(jnp.float32)
+        top, low = slice(f * 256, f * 256 + 128), slice(f * 256 + 128, f * 256 + 256)
         for c in range(TLEN // LANES + 1):
             if c < TLEN // LANES:
                 now = skew(rows[f % 2:f % 2 + 1, c * 128:(c + 1) * 128])
             else:
                 now = zero
-            ctab[f * 128:(f + 1) * 128, c * 128:(c + 1) * 128] = jnp.where(keep, now, last).astype(jnp.bfloat16)
+            tile = jnp.where(keep, now, last).astype(jnp.bfloat16)
             last = now
-
+            ctab[top, c * 128:(c + 1) * 128] = tile
+            ctab[low, (c + 1) * 128:(c + 2) * 128] = tile
+        ctab[top, 17 * 128:18 * 128] = zero_b
+        ctab[low, 0:128] = zero_b
+
+    tap_table()
+    tmpl_table(0)
+    tmpl_table(1)
     edge = jnp.where((y <= 1) | (y >= 6), NY, 0)
     pl.semaphore_wait(barrier, 29 + 2 * NZ + edge)
 
@@ -122,7 +129,14 @@
         send_a(jnp.where(
             x == 0, bank_of((y + jj) % NY, z, (x + dx) % NX), bank_of(y, (z + jj) % NZ, (x + dx) % NX)
         ))
-    tap_table()
+    tmpl_table(2)
+    tmpl_table(3)
+    inv = []
+    for k in range(2):
+        wide = tmpl_v[k].astype(jnp.float32)
+        energy = jnp.sum(wide * wide, keepdims=True) / (2.0 * TLEN) + 1e-6
+        inv.append(1.0 / (TLEN * energy))
+
     got = pairs.at[pl.ds(0, 15), 0, pl.ds(0, DET), :]
     pltpu.make_async_copy(got, got, recv_sem.at[0]).wait()
 
@@ -175,82 +189,79 @@
     margin_z(z < 4, 2, 1)
     margin_z(z >= 4, 1, 2)
 
-    for f in range(4):
-        tmpl_table(f)
-    inv = []
-    for k in range(2):
-        wide = tmpl_v[k].astype(jnp.float32)
-        energy = jnp.sum(wide * wide, keepdims=True) / (2.0 * TLEN) + 1e-6
-        inv.append(1.0 / (TLEN * energy))
-
     got = pairs.at[pl.ds(0, 80), :, pl.ds(0, DET), :]
     pltpu.make_async_copy(got, got, recv_sem.at[1]).wait()
 
     nt = (((1,), (1,)), ((), ()))
-    for a in range(WSTEP + WOFF - 1):
-        for d in range(DET):
-            rows = slice(a * ROWS + d * 16, a * ROWS + d * 16 + 16)
-            for h in range(2):
-                val = gath[pl.ds(8 * (2 * a + h) + d, 16, stride=16 * WSTEP), :]
-                hi = val.astype(jnp.bfloat16)
-                lo = (val - hi.astype(jnp.float32)).astype(jnp.bfloat16)
-                xh[rows, h * 128:(h + 1) * 128] = hi
-                xl[rows, h * 128:(h + 1) * 128] = lo
-    hi_all = jnp.concatenate([xh[o * ROWS:(o + WSTEP) * ROWS, :] for o in range(WOFF)], axis=1)
-    lo_all = jnp.concatenate([xl[o * ROWS:(o + WSTEP) * ROWS, :] for o in range(WOFF)], axis=1)
-    both = lax.dot_general(
-        jnp.concatenate([hi_all, lo_all], axis=0), wtab[0], nt, preferred_element_type=jnp.float32
-    )
-    out = both[:WSTEP * ROWS] + both[WSTEP * ROWS:]
-    out += lax.dot_general(hi_all, wtab[1], nt, preferred_element_type=jnp.float32)
+
+    @pl.when(b >= 0)
+    def _():
+        for a in range(WSTEP + WOFF - 1):
+            for d in range(DET):
+                rows = slice(a * ROWS + d * 16, a * ROWS + d * 16 + 16)
+                for h in range(2):
+                    val = gath[pl.ds(8 * (2 * a + h) + d, 16, stride=16 * WSTEP), :]
+                    hi = val.astype(jnp.bfloat16)
+                    lo = (val - hi.astype(jnp.float32)).astype(jnp.bfloat16)
+                    xh[rows, h * 128:(h + 1) * 128] = hi
+                    xl[rows, h * 128:(h + 1) * 128] = lo
+        hi_all = jnp.concatenate([xh[o * ROWS:(o + WSTEP) * ROWS, :] for o in range(WOFF)], axis=1)
+        lo_all = jnp.concatenate([xl[o * ROWS:(o + WSTEP) * ROWS, :] for o in range(WOFF)], axis=1)
+        both = lax.dot_general(
+            jnp.concatenate([hi_all, lo_all], axis=0), wtab[0], nt, preferred_element_type=jnp.float32
+        )
+        acc[...] = both[:WSTEP * ROWS] + both[WSTEP * ROWS:] + lax.dot_general(
+            hi_all, wtab[1], nt, preferred_element_type=jnp.float32
+        )
+
+    n_out = WSTEP * ROWS
+    out = acc[...]
+    n_more = (COFF - 1 - WSTEP) * ROWS
+    cwin[0:n_out, :] = out.astype(jnp.bfloat16)
+    cwin[n_out:2 * n_out, :] = pltpu.roll(out, n_out - 1, 0).astype(jnp.bfloat16)
+    cwin[2 * n_out:2 * n_out + n_more, :] = pltpu.roll(out, n_out - 2, 0)[:n_more].astype(jnp.bfloat16)
+    wins = jnp.concatenate([cwin[o * ROWS:o * ROWS + n_out, :] for o in range(COFF)], axis=1)
+    corr = lax.dot_general(wins, ctab[...], nt, preferred_element_type=jnp.float32)
+    power = []
+    for k in range(2):
+        c0 = corr[:, k * 512:k * 512 + 256]
+        c1 = corr[:, k * 512 + 256:k * 512 + 512]
+        power.append((c0 * c0 + c1 * c1) * inv[k])
+    best = jnp.maximum(power[0], power[1])
     for a in range(WSTEP):
         for d in range(DET):
             rows = slice(a * ROWS + d * 16, a * ROWS + d * 16 + 16)
             for h in range(2):
-                white[pl.ds(d * 160 + 2 * a + h, 16, stride=2 * WSTEP), :] = out[rows, h * 128:(h + 1) * 128]
-
-    for a in range(CSTEP + COFF - 1):
-        for d in range(DET):
-            rows = slice(a * ROWS + d * 16, a * ROWS + d * 16 + 16)
-            cwin[rows, :] = white[pl.ds(d * 160 + a, 16, stride=CSTEP), :].astype(jnp.bfloat16)
-    wins = jnp.concatenate([cwin[o * ROWS:(o + CSTEP) * ROWS, :] for o in range(COFF)], axis=1)
-    corr = lax.dot_general(wins, ctab[...], nt, preferred_element_type=jnp.float32)
-    power = []
-    for k in range(2):
-        c0 = corr[:, k * 256:k * 256 + 128]
-        c1 = corr[:, k * 256 + 128:k * 256 + 256]
-        power.append((c0 * c0 + c1 * c1) * inv[k])
-    best = jnp.maximum(power[0], power[1])
-    for a in range(CSTEP):
-        for d in range(DET):
-            rows = slice(a * ROWS + d * 16, a * ROWS + d * 16 + 16)
-            for k in range(2):
-                snr[pl.ds(d * 256 + 2 * a + k, 16, stride=16), :] = power[k][rows]
-            sbuf[pl.ds(8 * a + d, 16, stride=64), :] = best[rows]
-
-    send3 = sbuf.reshape(BANK, 8, LANES)
-
-    far = (4, 3, 5, 2, 6, 1, 7, 0)
-    zs = [((z + jz) % NZ) * 2 for jz in far]
+                sbuf[pl.ds(8 * (2 * a + h) + d, 16, stride=16 * WSTEP), :] = best[rows, h * 128:(h + 1) * 128]
+
+    send3 = sbuf.reshape(160, 8, LANES)
+
+    ys = [((y + j) % NY) * 16 for j in range(NY)]
+    zs = [((z + j) % NZ) * 2 for j in range(NZ)]
+    xs = [x, 1 - x]
+    steps = sorted(
+        ((2 * jx + min(jy, NY - jy) + min(jz, NZ - jz), jx, jy, jz)
+         for jx in range(NX) for jy in range(NY) for jz in range(NZ)), reverse=True
+    )[:BANK - 1]
 
     def to_all(make):
-        def some(i, carry):
-            jx, jy = 1 - i // 8, far_first(i % 8)
-            base = bank_of((y + jy) % NY, 0, (x + jx) % NX)
-            for n in range(8):
-                make(base + zs[n]).start()
-            return carry
-
-        lax.fori_loop(0, 15, some, 0)
-        base = bank_of(y, 0, x)
-        for n in range(7):
-            make(base + zs[n]).start()
+        for n, (hops, jx, jy, jz) in enumerate(steps):
+            make(ys[jy] + zs[jz] + xs[jx]).start()
 
     to_all(lambda p: pltpu.make_async_remote_copy(
         src_ref=send3.at[p, pl.ds(0, DET), :], dst_ref=rbuf.at[b, pl.ds(0, DET), :],
         send_sem=send_sem.at[2], recv_sem=recv_sem.at[2],
         device_id=(p, m), device_id_type=MESH,
     ))
+    for a in range(WSTEP):
+        count = (63 - a) // WSTEP + 1
+        for d in range(DET):
+            rows = slice(a * ROWS + d * 16, a * ROWS + d * 16 + count)
+            for h in range(2):
+                for k in range(2):
+                    snr[pl.ds(d * 256 + 2 * (2 * a + h) + k, count, stride=4 * WSTEP), :] = (
+                        power[k][rows, h * 128:(h + 1) * 128]
+                    )
     own = send3[b, 0:DET, :]
     got = rbuf.at[pl.ds(0, BANK - 1), pl.ds(0, DET), :]
     pltpu.make_async_copy(got, got, recv_sem.at[2]).wait()
@@ -259,11 +270,23 @@
     res[...] = top
     mine = pl.ds(pl.multiple_of(b * 128, 128), 128)
 
-    to_all(lambda p: pltpu.make_async_remote_copy(
-        src_ref=res, dst_ref=loud.at[:, mine],
-        send_sem=send_sem.at[3], recv_sem=recv_sem.at[3],
-        device_id=(p, m), device_id_type=MESH,
-    ))
+    def spread(p):
+        return pltpu.make_async_remote_copy(
+            src_ref=res, dst_ref=loud.at[:, mine],
+            send_sem=send_sem.at[3], recv_sem=recv_sem.at[3],
+            device_id=(p, m), device_id_type=MESH,
+        )
+
+    planes = sorted(
+        ((2 * jx + min(jy, NY - jy), jx, jy) for jx in range(NX) for jy in range(NY)), reverse=True
+    )
+    for zz in range(NZ):
+        for hops, jx, jy in planes:
+            copy = spread(ys[jy] + 2 * zz + xs[jx])
+            if hops:
+                copy.start()
+            else:
+                pl.when(z != zz)(copy.start)
     loud[:, mine] = top
     got = rbuf.at[pl.ds(0, BANK - 1), pl.ds(0, DET), :]
     pltpu.make_async_copy(got, got, recv_sem.at[3]).wait()
@@ -289,28 +312,40 @@
     pltpu.make_async_copy(sent, sent, send_sem.at[3]).wait()
 
 
+def place(snr_v, loud_v, snr, loud, sem):
+    copies = [
+        pltpu.make_async_copy(snr_v, snr, sem.at[0]),
+        pltpu.make_async_copy(loud_v, loud, sem.at[1]),
+    ]
+    for copy in copies:
+        copy.start()
+    for copy in copies:
+        copy.wait()
+
+
 def shards(strain, fir_taps, templates):
-    any_spec = pl.BlockSpec(memory_space=pltpu.HBM)
     vmem_spec = pl.BlockSpec(memory_space=pltpu.VMEM)
+    shapes = (
+        jax.ShapeDtypeStruct((DET * 256, LANES), jnp.float32),
+        jax.ShapeDtypeStruct((DET, BANK * LANES), jnp.float32),
+    )
+    hbm_spec = pl.BlockSpec(memory_space=pltpu.HBM)
     snr, loud = pl.pallas_call(
         kernel,
-        out_shape=(
-            jax.ShapeDtypeStruct((DET * 256, LANES), jnp.float32),
-            jax.ShapeDtypeStruct((DET, BANK * LANES), jnp.float32),
-        ),
-        in_specs=[any_spec, any_spec, any_spec],
+        out_shape=shapes,
+        in_specs=[hbm_spec, hbm_spec, hbm_spec],
         out_specs=(vmem_spec, vmem_spec),
         scratch_shapes=[
             pltpu.VMEM((96 * 16, LANES), jnp.float32),
             pltpu.VMEM((TAPS // LANES, LANES), jnp.float32),
             pltpu.VMEM((2, 2, TLEN), jnp.bfloat16),
             pltpu.VMEM((2, 256, WOFF * 256), jnp.bfloat16),
-            pltpu.VMEM((512, COFF * 128), jnp.bfloat16),
+            pltpu.VMEM((1024, COFF * 256), jnp.bfloat16),
             pltpu.VMEM(((WSTEP + WOFF - 1) * ROWS, 256), jnp.bfloat16),
             pltpu.VMEM(((WSTEP + WOFF - 1) * ROWS, 256), jnp.bfloat16),
-            pltpu.VMEM((DET * 160, LANES), jnp.float32),
-            pltpu.VMEM(((CSTEP + COFF - 1) * ROWS, LANES), jnp.bfloat16),
-            pltpu.VMEM((BANK * 8, LANES), jnp.float32),
+            pltpu.VMEM((WSTEP * ROWS, 256), jnp.float32),
+            pltpu.VMEM(((WSTEP + COFF - 1) * ROWS, 256), jnp.bfloat16),
+            pltpu.VMEM((160 * 8, LANES), jnp.float32),
             pltpu.VMEM((BANK, 8, LANES), jnp.float32),
             pltpu.VMEM((DET, LANES), jnp.float32),
             pltpu.SemaphoreType.DMA((3,)),
@@ -323,6 +358,15 @@
         ),
         name="matched_filter",
     )(*[pltpu.with_memory_space_constraint(v, pltpu.HBM) for v in (strain, fir_taps.reshape(TAPS // LANES, LANES), templates)])
+    snr, loud = pl.pallas_call(
+        place,
+        out_shape=shapes,
+        in_specs=[vmem_spec, vmem_spec],
+        out_specs=(hbm_spec, hbm_spec),
+        scratch_shapes=[pltpu.SemaphoreType.DMA((2,))],
+        compiler_params=pltpu.CompilerParams(vmem_limit_bytes=1024 * 1024),
+        name="place",
+    )(snr, loud)
     snr = snr.reshape(DET, 128, 2, LANES).transpose(0, 2, 1, 3).reshape(DET, 2, 128 * LANES)
     return snr, loud
 

time: 51.9 us -> 49.7 us (0.958)
  local copies, waits for them, and re-layouts: 1.45 us -> 0 us
  Pallas kernels: 49.6 us -> 48.9 us
    unnamed x2 -> x0, local copies, waits for them, and re-layouts: 1.45 us -> none
    pallas_call x1 -> x2, Pallas kernels: 49.6 us -> 48.9 us  [the longest x1 48.1 us: shards(): pl.pallas_call(kernel, out_shape=shapes, in_specs=[hbm_spec, hbm_spec, hb...]
where the time goes in v3:
time: 49.7 us; the launch traced here: 49.5 us
  Pallas kernels  48.9 us (98%)
  between operations  0.64 us (1%)
    pallas_call x1, Pallas kernels, shards(): pl.pallas_call(kernel, out_shape=shapes, in_specs=[hbm_spec, hbm_spec, hb...  48.1 us

profile of v3, /device:TPU:1, one launch (start us, length us, event | category | flops | bytes accessed | tf_op | source)
XLA Modules:
  0.0 49.5 jit_solution(6559646490181357742)
XLA Ops:
  0.6 48.1 %matched_filter.1 = (f32[768,128]{1,0:T(8,128)S(1)}, f32[3,16384]{1,0:T(4,128)S(1)}) custom-call(f32[3,1,128]{2,1,0:T(1,128)} %strain.1, f32[32,128]{1,0:T(8,128)} %bitcast.6, bf16[2,2,2048]{2,1,0:T(2,128)(2,1)} %tmpl.1), custom_call_target="tpu_custom_call" | custom-call | tf_op jit(solution)/shard_map/matched_filter/pallas_call | solution.py:333
  48.7 0.9 %place.1 = (f32[768,128]{1,0:T(8,128)}, f32[3,16384]{1,0:T(4,128)}) custom-call(f32[768,128]{1,0:T(8,128)S(1)} %get-tuple-element.6.snr_v, f32[3,16384]{1,0:T(4,128)S(1)} %get-tuple-element.7.loud_v), custom_call_target="tpu_custom_call" | custom-call | tf_op jit(solution)/shard_map/place/pallas_call | solution.py:361

commit v4 on v3

--- a/solution.py
+++ b/solution.py
@@ -150,11 +150,6 @@
     at_q, at_r = (12 + z) // 8, (z + 4) % 8
     yline = eights.at[pl.ds(at_q, 8), at_r, 0, pl.ds(0, DET), :]
     zline = pairs.at[pl.ds(12 + 8 * y, 8), 1, pl.ds(0, DET), :]
-    for j in range(7):
-        jj = far_first(j)
-        send_b(yline, yline, send_sem.at[1], bank_of(y, (z + jj) % NZ, x), m)
-        send_b(zline, zline, send_sem.at[1], bank_of((y + jj) % NY, z, x), m)
-
     def margin_y(cond, src_at, dst_at, count, to):
         @pl.when(cond)
         def _():
@@ -188,6 +183,11 @@
 
     margin_z(z < 4, 2, 1)
     margin_z(z >= 4, 1, 2)
+
+    for j in range(7):
+        send_b(zline, zline, send_sem.at[1], bank_of((y + far_first(j)) % NY, z, x), m)
+    for j in range(7):
+        send_b(yline, yline, send_sem.at[1], bank_of(y, (z + far_first(j)) % NZ, x), m)
 
     got = pairs.at[pl.ds(0, 80), :, pl.ds(0, DET), :]
     pltpu.make_async_copy(got, got, recv_sem.at[1]).wait()

time: 49.7 us -> 48.3 us (0.972)
  Pallas kernels: 48.9 us -> 47.5 us
    pallas_call x1, Pallas kernels: 48.1 us -> 46.6 us  [shards(): pl.pallas_call(kernel, out_shape=shapes, in_specs=[hbm_spec, hbm_spec, hb...]
where the time goes in v4:
time: 48.3 us; the launch traced here: 48.1 us
  Pallas kernels  47.5 us (98%)
  between operations  0.64 us (1%)
    pallas_call x1, Pallas kernels, shards(): pl.pallas_call(kernel, out_shape=shapes, in_specs=[hbm_spec, hbm_spec, hb...  46.6 us

profile of v4, /device:TPU:1, one launch (start us, length us, event | category | flops | bytes accessed | tf_op | source)
XLA Modules:
  0.0 48.1 jit_solution(5817589990043682949)
XLA Ops:
  0.6 46.6 %matched_filter.1 = (f32[768,128]{1,0:T(8,128)S(1)}, f32[3,16384]{1,0:T(4,128)S(1)}) custom-call(f32[3,1,128]{2,1,0:T(1,128)} %strain.1, f32[32,128]{1,0:T(8,128)} %bitcast.6, bf16[2,2,2048]{2,1,0:T(2,128)(2,1)} %tmpl.1), custom_call_target="tpu_custom_call" | custom-call | tf_op jit(solution)/shard_map/matched_filter/pallas_call | solution.py:333
  47.3 0.9 %place.1 = (f32[768,128]{1,0:T(8,128)}, f32[3,16384]{1,0:T(4,128)}) custom-call(f32[768,128]{1,0:T(8,128)S(1)} %get-tuple-element.6.snr_v, f32[3,16384]{1,0:T(4,128)S(1)} %get-tuple-element.7.loud_v), custom_call_target="tpu_custom_call" | custom-call | tf_op jit(solution)/shard_map/place/pallas_call | solution.py:361

commit v5 on v4

--- a/solution.py
+++ b/solution.py
@@ -16,6 +16,7 @@
 WOFF = 17
 COFF = 9
 ROWS = 16 * DET
+SNR_ROWS = 832
 
 
 def far_first(i):
@@ -60,7 +61,7 @@
     own_row = pairs.at[12 + 8 * y + z, x, pl.ds(0, DET), :]
     load_own = pltpu.make_async_copy(strain.at[:, 0, :], own_row, in_sem.at[0])
     load_taps = pltpu.make_async_copy(taps, tap_v, in_sem.at[1])
-    load_tmpl = pltpu.make_async_copy(tmpl, tmpl_v, in_sem.at[2])
+    load_tmpl = pltpu.make_async_copy(tmpl, tmpl_v.at[pl.ds(0, 2)], in_sem.at[2])
     load_own.start()
     load_taps.start()
     load_tmpl.start()
@@ -267,12 +268,13 @@
     pltpu.make_async_copy(got, got, recv_sem.at[2]).wait()
     rbuf[b, 0:DET, :] = own
     top = jnp.max(rbuf[:, 0:DET, :], axis=0)
-    res[...] = top
+    res[0:DET, :] = top
+    final = res.at[pl.ds(0, DET), :]
     mine = pl.ds(pl.multiple_of(b * 128, 128), 128)
 
     def spread(p):
         return pltpu.make_async_remote_copy(
-            src_ref=res, dst_ref=loud.at[:, mine],
+            src_ref=final, dst_ref=loud.at[:, mine],
             send_sem=send_sem.at[3], recv_sem=recv_sem.at[3],
             device_id=(p, m), device_id_type=MESH,
         )
@@ -287,7 +289,9 @@
                 copy.start()
             else:
                 pl.when(z != zz)(copy.start)
-    loud[:, mine] = top
+    keep_own = pltpu.make_async_copy(final, loud.at[:, mine], in_sem.at[1])
+    keep_own.start()
+    keep_own.wait()
     got = rbuf.at[pl.ds(0, BANK - 1), pl.ds(0, DET), :]
     pltpu.make_async_copy(got, got, recv_sem.at[3]).wait()
     sent = pairs.at[pl.ds(0, 15), 0, pl.ds(0, DET), :]
@@ -314,7 +318,7 @@
 
 def place(snr_v, loud_v, snr, loud, sem):
     copies = [
-        pltpu.make_async_copy(snr_v, snr, sem.at[0]),
+        pltpu.make_async_copy(snr_v.at[pl.ds(0, DET * 256), :], snr, sem.at[0]),
         pltpu.make_async_copy(loud_v, loud, sem.at[1]),
     ]
     for copy in copies:
@@ -332,13 +336,13 @@
     hbm_spec = pl.BlockSpec(memory_space=pltpu.HBM)
     snr, loud = pl.pallas_call(
         kernel,
-        out_shape=shapes,
+        out_shape=(jax.ShapeDtypeStruct((SNR_ROWS, LANES), jnp.float32), shapes[1]),
         in_specs=[hbm_spec, hbm_spec, hbm_spec],
         out_specs=(vmem_spec, vmem_spec),
         scratch_shapes=[
             pltpu.VMEM((96 * 16, LANES), jnp.float32),
             pltpu.VMEM((TAPS // LANES, LANES), jnp.float32),
-            pltpu.VMEM((2, 2, TLEN), jnp.bfloat16),
+            pltpu.VMEM((4, 2, TLEN), jnp.bfloat16),
             pltpu.VMEM((2, 256, WOFF * 256), jnp.bfloat16),
             pltpu.VMEM((1024, COFF * 256), jnp.bfloat16),
             pltpu.VMEM(((WSTEP + WOFF - 1) * ROWS, 256), jnp.bfloat16),
@@ -347,7 +351,7 @@
             pltpu.VMEM(((WSTEP + COFF - 1) * ROWS, 256), jnp.bfloat16),
             pltpu.VMEM((160 * 8, LANES), jnp.float32),
             pltpu.VMEM((BANK, 8, LANES), jnp.float32),
-            pltpu.VMEM((DET, LANES), jnp.float32),
+            pltpu.VMEM((8, LANES), jnp.float32),
             pltpu.SemaphoreType.DMA((3,)),
             pltpu.SemaphoreType.DMA((4,)),
             pltpu.SemaphoreType.DMA((4,)),

time: 48.3 us -> 48.3 us (level)
  no operation moved by 1% of the time
where the time goes in v5:
time: 48.3 us; the launch traced here: 48.1 us
  Pallas kernels  47.4 us (98%)
  between operations  0.64 us (1%)
    pallas_call x1, Pallas kernels, shards(): pl.pallas_call(kernel, out_shape=(jax.ShapeDtypeStruct((SNR_ROWS, LANES),...  46.6 us

profile of v5, /device:TPU:1, one launch (start us, length us, event | category | flops | bytes accessed | tf_op | source)
XLA Modules:
  0.0 48.1 jit_solution(18265583227293908571)
XLA Ops:
  0.6 46.6 %matched_filter.1 = (f32[832,128]{1,0:T(8,128)S(1)}, f32[3,16384]{1,0:T(4,128)S(1)}) custom-call(f32[3,1,128]{2,1,0:T(1,128)} %strain.1, f32[32,128]{1,0:T(8,128)} %bitcast.6, bf16[2,2,2048]{2,1,0:T(2,128)(2,1)} %tmpl.1), custom_call_target="tpu_custom_call" | custom-call | tf_op jit(solution)/shard_map/matched_filter/pallas_call | solution.py:337
  47.2 0.9 %place.1 = (f32[768,128]{1,0:T(8,128)}, f32[3,16384]{1,0:T(4,128)}) custom-call(f32[832,128]{1,0:T(8,128)S(1)} %get-tuple-element.6.snr_v, f32[3,16384]{1,0:T(4,128)S(1)} %get-tuple-element.7.loud_v), custom_call_target="tpu_custom_call" | custom-call | tf_op jit(solution)/shard_map/place/pallas_call | solution.py:365
